TPU v7x, 128 devices: a whole 4x4x4 slice. The times are simulated.
128 devices in a mesh: freq: 32 (over y, x_lo, z), pair: 4 (over x_hi, core).
Axes of the slice: x: 4 (x_hi: 2, x_lo: 2; x = x_hi * 2 + x_lo), y: 4, z: 4, core: 2. Of those that a mesh axis runs over, the one named last changes fastest.
Arguments:
- vertex: float32 [64, 2, 48, 48, 1024], P('freq', None, None, None, 'pair'), may hold values from -6 to 6
- bubble: float32 [64, 48], P('freq'), may hold values from 0.02 to 0.2
- stencil: float32 [64, 5], P('freq'), may hold values from -3 to 3
- freq_map: int32 [48], replicated, may hold values from 0 to 47
- neighbours: int32 [8192, 3], replicated, may hold values from -1 to 1023, as said below
Outputs:
- section_vertex: float32 [64, 2, 48, 48, 1024], P('freq', None, None, None, 'pair')
Inputs may be any that keep to these rules, and one draw needn't show every extreme that they name: `neighbours`: each pair index 0 to 1023 stands in column 0 of exactly 8 rows; column 1 holds any pair index; column 2 is -1 or 1.
All inputs are finite; a program needn't handle non-finite values.
Results may differ from a plain program's by a relative error of at most 0.0003.
Values sent between devices are 32-bit elements; how exact they have to be, the bound alone decides.
No kernel may reach another device: no remote copies, remote signals or barrier semaphores. Data moves between devices by JAX's collectives and lax.ppermute only.
A program may use at most 320 MiB of HBM per device.

v0:
```python
import jax
import jax.numpy as jnp
from jax import lax
from jax.sharding import PartitionSpec as P

step_size = 0.25
highest = lax.Precision.HIGHEST


def padded_2(cells, sides, width):
    for axis, dim in sides:
        count = lax.axis_size(axis)
        ends = count - 1
        head = lax.slice_in_dim(cells, 0, width, axis=dim)
        tail = lax.slice_in_dim(cells, cells.shape[dim] - width, cells.shape[dim], axis=dim)
        cells = jnp.concatenate(
            [
                lax.ppermute(tail, axis, [(i, (i + 1) % count) for i in range(ends)]),
                cells,
                lax.ppermute(head, axis, [((i + 1) % count, i) for i in range(ends)]),
            ],
            axis=dim,
        )
    return cells


def pair_matrix(neighbours, left_count, first_right, right_count):
    pair_column = neighbours[:, 0]
    partner_column = neighbours[:, 1]
    sign_column = neighbours[:, 2]
    left_ids = lax.iota(jnp.int32, left_count)
    right_ids = first_right + lax.iota(jnp.int32, right_count)
    partner_hits = (partner_column[:, None] == left_ids[None, :]).astype(jnp.bfloat16)
    pair_hits = jnp.where(
        pair_column[:, None] == right_ids[None, :], sign_column[:, None], 0
    ).astype(jnp.bfloat16)
    return lax.dot_general(
        partner_hits, pair_hits, (((0,), (0,)), ((), ())), preferred_element_type=jnp.float32
    )


def lattice_sum(spin_part, neighbours):
    pair_count = spin_part.shape[3]
    shards = lax.axis_size("pair")
    all_pairs = pair_count * shards
    position = lax.axis_index("pair") * pair_count
    coupling = pair_matrix(neighbours, all_pairs, position, pair_count)
    return jnp.einsum(
        "snwq,qp->snwp",
        lax.all_gather(spin_part, "pair", axis=3, tiled=True),
        coupling,
        precision=highest,
    )


def widen(vertex):
    return padded_2(vertex, (("freq", 0),), 2)


def body(vertex, bubble, stencil, freq_map, neighbours):
    padded = widen(vertex)
    lattice = lattice_sum(vertex[:, 0], neighbours)
    slot_count = vertex.shape[0]
    mixed = jnp.zeros_like(vertex)
    for offset in range(5):
        mixed = (
            mixed
            + stencil[:, offset][:, None, None, None, None] * padded[offset : offset + slot_count]
        )
    width = vertex.shape[2]
    selector = (freq_map[:, None] == lax.iota(jnp.int32, width)[None, :]).astype(jnp.float32)
    mapped = jnp.einsum("nm,scmwp->scnwp", selector, mixed, precision=highest)
    weighted = mapped * bubble[:, None, None, :, None]
    crossed = jnp.einsum("scnwp,scwmp->scnmp", weighted, vertex, precision=highest)
    spin_part = vertex[:, 0]
    lattice_term = jnp.einsum(
        "snwp,swmp->snmp", lattice * bubble[:, None, :, None], spin_part, precision=highest
    )
    deriv = crossed.at[:, 0].add(-lattice_term)
    return vertex + step_size * deriv


def solution(mesh):
    in_specs = (P("freq", None, None, None, "pair"), P("freq", None), P("freq", None), P(), P())
    out_specs = P("freq", None, None, None, "pair")
    return jax.shard_map(body, mesh=mesh, in_specs=in_specs, out_specs=out_specs, check_vma=False)
```

profile of v0, /device:TPU:24, one launch (start us, length us, event | category | flops | bytes accessed | tf_op | source)
XLA Modules:
  0.0 718.7 jit_solution(16640508304583043875)
XLA Ops:
  6.5 0.0 all-gather.3.cloned.1.call-start
  6.5 4.9 slice.79
  11.4 10.8 %copy.21 = f32[2,1,48,48,256]{3,2,4,0,1:T(8,128)} copy(f32[2,1,48,48,256]{4,3,2,1,0:T(8,128)} %slice.79) | data formatting | bytes 9437184
  22.2 0.0 all-gather.3.cloned.1.call-update
  22.2 7.1 collective-permute-start.1
  29.2 1.9 collective-permute-start
  31.2 0.0 copy-start.2
  31.2 0.0 copy-start.1
  31.2 20.7 %copy.10 = f32[2,2,48,48,256]{3,2,4,1,0:T(8,128)} copy(f32[2,2,48,48,256]{4,3,2,1,0:T(8,128)} %param.7) | data formatting | bytes 18874368 | tf_op args[0]
  51.9 0.0 copy-done.2
  51.9 0.2 slice_reduce_fusion.4
  52.1 0.0 copy-done.1
  52.1 0.1 fusion.32
  52.2 12.1 %fusion.27 = f32[1024,256,1,1]{1,0,3,2:T(8,128)S(1)} fusion(s32[8192]{0:T(1024)S(1)} %bitcast.38, s32[256]{0:T(256)S(1)} %iota_add_fusion, s32[8192]{0:T(1024)S(1)} %bitcast.39, s32[8192]{0:T(1024)S(1)} %bitcast.37), kind=kOutput, calls=%fused_computation.33 | convolution fusion | flops 4309647360 | bytes 1147904 | tf_op jit(solution)/shard_map/dot_general | solution.py:37
  64.3 350.1 %collective-permute-done.1 = f32[2,2,48,48,256]{4,3,2,1,0:T(8,128)} collective-permute-done((f32[2,2,48,48,256]{4,3,2,1,0:T(8,128)}, f32[2,2,48,48,256]{4,3,2,1,0:T(8,128)}, u32[]{:S(2)}, u32[]{:S(2)}) %collective-permute-start.1) | collective-permute-done | bytes 9437216 | tf_op jit(solution)/shard_map/ppermute | solution.py:20
  414.4 10.0 %collective-permute-done = f32[2,2,48,48,256]{4,3,2,1,0:T(8,128)} collective-permute-done((f32[2,2,48,48,256]{4,3,2,1,0:T(8,128)}, f32[2,2,48,48,256]{4,3,2,1,0:T(8,128)}, u32[]{:S(2)}, u32[]{:S(2)}) %collective-permute-start) | collective-permute-done | bytes 9437216 | tf_op jit(solution)/shard_map/ppermute | solution.py:18
  424.4 0.0 copy-start.3
  424.4 17.8 %fusion.14 = f32[2,2,48,48,256]{4,3,2,1,0:T(8,128)S(1)} fusion(f32[2,2,48,48,256]{4,3,2,1,0:T(8,128)} %collective-permute-done.1, f32[2,2,48,48,256]{4,3,2,1,0:T(8,128)} %param.7, f32[2,2,48,48,256]{4,3,2,1,0:T(8,128)} %collective-permute-done, f32[2]{0:T(128)S(1)} %get-tuple-element.20, f32[2]{0:T(128)S(1)} %get-tuple-element.21, ...), kind=kLoop, calls=%fused_computation.16 | loop fusion | flops 25952256 | bytes 37748776 | tf_op jit(solution)/shard_map/add | solution.py:67
  442.2 0.0 copy-done.3
  442.2 11.4 %fusion.18 = f32[2,2,48,256,48]{3,4,2,1,0:T(8,128)} fusion(f32[2,2,48,48,256]{4,3,2,1,0:T(8,128)S(1)} %fusion.14, s32[48]{0:T(128)S(1)} %copy-done.3), kind=kOutput, calls=%fused_computation.21 | convolution fusion | flops 1358956800 | bytes 18874560 | tf_op jit(solution)/shard_map/nm,scmwp->scnwp/dot_general | solution.py:72
  453.6 0.0 copy-start
  453.6 20.5 %copy.17 = f32[2,2,48,256,48]{2,4,3,1,0:T(8,128)} copy(f32[2,2,48,256,48]{3,4,2,1,0:T(8,128)} %fusion.18) | data formatting | bytes 18874368 | tf_op jit(solution)/shard_map/nm,scmwp->scnwp/dot_general | solution.py:72
  474.1 0.0 copy-done
  474.1 33.8 %fusion.3 = f32[2,2,256,48,48]{4,3,2,1,0:T(8,128)} fusion(f32[2,2,48,48,256]{3,2,4,1,0:T(8,128)} %copy.10, f32[2,2,48,256,48]{2,4,3,1,0:T(8,128)} %copy.17, f32[2,48]{1,0:T(2,128)S(1)} %copy-done), kind=kOutput, calls=%fused_computation.4 | convolution fusion | flops 1361313792 | bytes 28311936 | tf_op jit(solution)/shard_map/scnwp,scwmp->scnmp/dot_general | solution.py:74
  507.9 20.0 %copy.11 = f32[2,2,256,48,48]{2,4,3,1,0:T(8,128)} copy(f32[2,2,256,48,48]{4,3,2,1,0:T(8,128)} %fusion.3) | data formatting | bytes 18874368 | tf_op jit(solution)/shard_map/scnwp,scwmp->scnmp/dot_general | solution.py:74
  527.9 8.1 %copy.26 = f32[2,2,48,48,256]{4,3,2,1,0:T(8,128)} copy(f32[2,2,48,48,256]{4,3,2,1,0:T(8,128)} %bitcast.36) | data formatting | bytes 18874368
  536.1 115.0 %fusion = f32[256,2,48,48]{0,3,2,1:T(8,128)} fusion(f32[1024,256,1,1]{1,0,3,2:T(8,128)S(1)} %fusion.27, f32[2,48,48,1024]{2,1,3,0:T(8,128)} %bitcast.35), kind=kOutput, calls=%fused_computation | convolution fusion | flops 14495514624 | bytes 24641536 | tf_op jit(solution)/shard_map/snwq,qp->snwp/dot_general | solution.py:48
  651.1 10.8 %copy.20 = f32[256,2,48,48]{3,2,0,1:T(8,128)} copy(f32[256,2,48,48]{0,3,2,1:T(8,128)} %fusion) | data formatting | bytes 9437184 | tf_op jit(solution)/shard_map/snwq,qp->snwp/dot_general | solution.py:48
  661.9 19.6 %fusion.7 = f32[2,256,48,48]{3,2,1,0:T(8,128)} fusion(f32[2,1,48,48,256]{3,2,4,0,1:T(8,128)} %copy.21, f32[256,2,48,48]{3,2,0,1:T(8,128)} %copy.20, f32[2,48]{1,0:T(2,128)S(1)} %copy-done), kind=kOutput, calls=%fused_computation.8 | convolution fusion | flops 680656896 | bytes 14156160 | tf_op jit(solution)/shard_map/snwp,swmp->snmp/dot_general | solution.py:76
  681.5 10.7 %copy.14 = f32[2,256,48,48]{1,3,2,0:T(8,128)} copy(f32[2,256,48,48]{3,2,1,0:T(8,128)} %fusion.7) | data formatting | bytes 9437184 | tf_op jit(solution)/shard_map/snwp,swmp->snmp/dot_general | solution.py:76
  692.2 6.9 fusion.22
  699.1 12.4 %multiply_add_fusion = f32[2,2,48,48,256]{4,3,2,1,0:T(8,128)} fusion(f32[2,2,48,48,256]{4,3,2,1,0:T(8,128)} %param.7, f32[2,2,48,48,256]{4,3,2,1,0:T(8,128)} %fusion.22), kind=kLoop, calls=%fused_computation.23 | loop fusion | flops 4718592 | bytes 28311552 | tf_op jit(solution)/shard_map/add | solution.py:80
  (2 shorter events, 0.0 us)
Async XLA Ops:
  6.5 529.5 %all-gather.3.cloned.1.call-start = ((), (), s32[]{:S(2)}) async-start(), calls=%async_computation | async-start | bytes 62914560 | tf_op jit(solution)/shard_map/all_gather | solution.py:50
  22.2 392.2 %collective-permute-start.1 = (f32[2,2,48,48,256]{4,3,2,1,0:T(8,128)}, f32[2,2,48,48,256]{4,3,2,1,0:T(8,128)}, u32[]{:S(2)}, u32[]{:S(2)}) collective-permute-start(f32[2,2,48,48,256]{4,3,2,1,0:T(8,128)} %param.7), channel_id=1, source_target_pairs={{4,0},{8,4},{12,8},{16,12},{20,16},{24,20},{28,24},{32,28},{36,32}... | collective-permute-start | bytes 28311560 | tf_op jit(solution)/shard_map/ppermute | solution.py:20
  29.2 395.2 %collective-permute-start = (f32[2,2,48,48,256]{4,3,2,1,0:T(8,128)}, f32[2,2,48,48,256]{4,3,2,1,0:T(8,128)}, u32[]{:S(2)}, u32[]{:S(2)}) collective-permute-start(f32[2,2,48,48,256]{4,3,2,1,0:T(8,128)} %param.7), channel_id=1, source_target_pairs={{0,4},{4,8},{8,12},{12,16},{16,20},{20,24},{24,28},{28,32},{32,36}... | collective-permute-start | bytes 28311560 | tf_op jit(solution)/shard_map/ppermute | solution.py:18
  31.2 20.7 %copy-start.2 = (f32[2,5]{1,0:T(2,128)S(1)}, f32[2,5]{1,0:T(2,128)}, u32[]{:S(2)}) copy-start(f32[2,5]{1,0:T(2,128)} %param.9) | copy-start | bytes 124
  31.2 20.9 %copy-start.1 = (s32[8192,3]{0,1:T(4,128)S(1)}, s32[8192,3]{0,1:T(4,128)}, u32[]{:S(2)}) copy-start(s32[8192,3]{0,1:T(4,128)} %param.11) | copy-start | bytes 294916
  424.4 17.8 %copy-start.3 = (s32[48]{0:T(128)S(1)}, s32[48]{0:T(128)}, u32[]{:S(2)}) copy-start(s32[48]{0:T(128)} %param.10) | copy-start | bytes 580
  453.6 20.5 %copy-start = (f32[2,48]{1,0:T(2,128)S(1)}, f32[2,48]{1,0:T(2,128)}, u32[]{:S(2)}) copy-start(f32[2,48]{1,0:T(2,128)} %param.8) | copy-start | bytes 1156
Sparse Core Ops, SparseCore 0:
  22.3 485.7 all-gather.2
where the time goes:
time: 730 us; the launch traced here: 719 us
  waiting for transfers between devices  360 us (49%)
  matrix products  192 us (26%)
  local copies, waits for them, and re-layouts  107 us (15%)
  other arithmetic  37 us (5%)
  between operations  13.9 us (2%)
  starting transfers between devices  8.98 us (1%)
    ppermute x1, waiting for transfers between devices, padded_2(): lax.ppermute(head, axis, [((i + 1) % count, i) for i in range(ends)])  350 us
    dot_general x1, matrix products, lattice_sum(): jnp.einsum('snwq,qp->snwp', lax.all_gather(spin_part, 'pair', axis=3, til...  115 us
    unnamed x11, local copies, waits for them, and re-layouts  39.5 us
    dot_general x1, matrix products, body(): jnp.einsum('scnwp,scwmp->scnmp', weighted, vertex, precision=highest)  33.8 us
    dot_general x1, local copies, waits for them, and re-layouts, body(): mapped = jnp.einsum('nm,scmwp->scnwp', selector, mixed, precision=highest)  20.5 us
    dot_general x1, local copies, waits for them, and re-layouts, body(): jnp.einsum('scnwp,scwmp->scnmp', weighted, vertex, precision=highest)  20 us
    dot_general x1, matrix products, body(): jnp.einsum('snwp,swmp->snmp', lattice * bubble[:, None, :, None], spin_pa...  19.6 us
    add x1, other arithmetic, body(): mixed + stencil[:, offset][:, None, None, None, None] * padded[offset:off...  17.8 us
  transfers between devices with their start and end apart: 3, of which 2 were waited for; matrix products, arithmetic and copies ran while one was open for 20% of the time, Pallas kernels for 0%

commit v1 on v0

v1 whole, which is shorter than its diff:
```python
import functools
import jax
import jax.numpy as jnp
from jax import lax
from jax.experimental import pallas as pl
from jax.experimental.pallas import tpu as pltpu
from jax.sharding import PartitionSpec as P

step_size = 0.25
lanes = 128
sublanes = 8
row_group = 8
vmem_bytes = 48 * 1024 * 1024


def cost(microseconds):
    return pl.CostEstimate(
        flops=0, bytes_accessed=int(microseconds * 3.0e6), transcendentals=0
    )


def contract(left, right, first, write):
    depth = right.shape[0]
    tiles = right.shape[1] // sublanes
    sums = [[None] * tiles for _ in range(row_group)]
    for w in range(depth):
        columns = [right[w, sublanes * t : sublanes * (t + 1), :] for t in range(tiles)]
        for i in range(row_group):
            row = jnp.broadcast_to(left[first + i, w : w + 1, :], (sublanes, lanes))
            for t in range(tiles):
                term = row * columns[t]
                sums[i][t] = term if w == 0 else sums[i][t] + term
    for i in range(row_group):
        for t in range(tiles):
            write(i, t, sums[i][t])


def pack_kernel(rows, vertex, packed):
    def one(u, carry):
        packed[0, u] = vertex[0, 0, rows[u]]
        return carry

    lax.fori_loop(0, packed.shape[1], one, 0)


def pack(vertex, rows, component, half):
    slots, _, width, depth, _ = vertex.shape
    count = rows.shape[0]
    return pl.pallas_call(
        pack_kernel,
        grid_spec=pltpu.PrefetchScalarGridSpec(
            num_scalar_prefetch=1,
            grid=(slots,),
            in_specs=[
                pl.BlockSpec((1, 1, width, depth, lanes), lambda s, r: (s, component, 0, 0, half))
            ],
            out_specs=pl.BlockSpec((1, count, depth, lanes), lambda s, r: (s, 0, 0, 0)),
        ),
        out_shape=jax.ShapeDtypeStruct((slots, count, depth, lanes), jnp.float32),
        compiler_params=pltpu.CompilerParams(vmem_limit_bytes=vmem_bytes),
        cost_estimate=cost(3),
        name="pack",
    )(rows, vertex)


def lattice_kernel(own, partner_1, partner_2, partner_3, coupling, bubble, spin, base, out, held):
    del base
    rows, depth, pairs = held.shape
    total = jnp.zeros((rows * depth, pairs), jnp.float32)
    for j, part in enumerate((own, partner_1, partner_2, partner_3)):
        block = part[...].reshape(rows * depth, pairs)
        high = block.astype(jnp.bfloat16)
        low = (block - high.astype(jnp.float32)).astype(jnp.bfloat16)
        matrix = coupling[j]
        total = total + jnp.dot(high, matrix, preferred_element_type=jnp.float32)
        total = total + jnp.dot(low, matrix, preferred_element_type=jnp.float32)
    held[...] = total.reshape(rows, depth, pairs)
    row_0 = pl.program_id(0) * rows
    for half in range(pairs // lanes):
        columns = pl.ds(half * lanes, lanes)
        for i in range(rows):
            held[i, :, columns] = held[i, :, columns] * bubble[0]

        def write(i, t, value, columns=columns):
            tile = pl.ds(sublanes * t, sublanes)
            out[0, 0, i, tile, columns] = spin[0, 0, row_0 + i, tile, columns] - value

        contract(held.at[:, :, columns], spin.at[0, 0, :, :, columns], 0, write)


def lattice(vertex, slot, partners, coupling, bubble, base):
    slots, components, width, depth, pairs = vertex.shape
    part = pl.BlockSpec((row_group, depth, pairs), lambda j: (j, 0, 0))
    return pl.pallas_call(
        lattice_kernel,
        grid=(width // row_group,),
        in_specs=[
            pl.BlockSpec((None, None, row_group, depth, pairs), lambda j: (slot, 0, j, 0, 0)),
            part,
            part,
            part,
            pl.BlockSpec(coupling.shape, lambda j: (0, 0, 0)),
            pl.BlockSpec((1, depth, lanes), lambda j: (slot, 0, 0)),
            pl.BlockSpec((1, 1, width, depth, pairs), lambda j: (slot, 0, 0, 0, 0)),
            pl.BlockSpec(memory_space=pl.ANY),
        ],
        out_specs=pl.BlockSpec((1, 1, row_group, depth, pairs), lambda j: (slot, 0, j, 0, 0)),
        out_shape=jax.ShapeDtypeStruct(vertex.shape, jnp.float32),
        scratch_shapes=[pltpu.VMEM((row_group, depth, pairs), jnp.float32)],
        input_output_aliases={7: 0},
        compiler_params=pltpu.CompilerParams(vmem_limit_bytes=vmem_bytes),
        cost_estimate=cost(10),
        name="lattice",
    )(vertex, *partners, coupling, bubble, vertex, base)


def crossed_kernel(has_base, rows, places, stencil, vertex, before, after, bubble, *rest):
    base = rest[0]
    out, weighted, result = rest[-3:]
    slot = pl.program_id(0)
    count, depth, _ = weighted.shape
    scale = bubble[0]

    def weigh(s):
        def one(u, carry):
            row = rows[u]
            sources = (
                before[0, u],
                before[1, u],
                vertex[0, 0, row],
                vertex[1, 0, row],
                after[0, u],
                after[1, u],
            )
            mixed = stencil[s, 0] * sources[s]
            for k in range(1, 5):
                mixed = mixed + stencil[s, k] * sources[s + k]
            weighted[u] = mixed * scale
            return carry

        lax.fori_loop(0, count, one, 0)

    for s in range(2):
        pl.when(slot == s)(functools.partial(weigh, s))

    current = vertex.at[slot, 0]

    def group(j, carry):
        first = j * row_group

        def write(i, t, value):
            result[first + i, sublanes * t : sublanes * (t + 1), :] = value

        contract(weighted, current, first, write)
        return carry

    lax.fori_loop(0, count // row_group, group, 0)

    def spread(n, carry):
        start = base[0, 0, n] if has_base else current[n]
        out[0, 0, n] = start + result[places[n]]
        return carry

    lax.fori_loop(0, out.shape[2], spread, 0)


def crossed(vertex, rows, places, stencil, before, after, bubble, component, half, has_base, base):
    slots, _, width, depth, _ = vertex.shape
    count = rows.shape[0]
    whole = pl.BlockSpec((slots, count, depth, lanes), lambda s, r, q: (0, 0, 0, 0))
    block = pl.BlockSpec(
        (1, 1, width, depth, lanes), lambda s, r, q: (s, component, 0, 0, half)
    )
    held = [block if has_base else pl.BlockSpec(memory_space=pl.ANY)]
    operands = (rows, places, stencil, vertex, before, after, bubble, base)
    if base is None:
        held, operands = [], operands[:-1]
    return pl.pallas_call(
        functools.partial(crossed_kernel, has_base),
        grid_spec=pltpu.PrefetchScalarGridSpec(
            num_scalar_prefetch=2,
            grid=(slots,),
            in_specs=[
                pl.BlockSpec(memory_space=pltpu.SMEM),
                pl.BlockSpec(
                    (slots, 1, width, depth, lanes), lambda s, r, q: (0, component, 0, 0, half)
                ),
                whole,
                whole,
                pl.BlockSpec((1, depth, lanes), lambda s, r, q: (s, 0, 0)),
                *held,
            ],
            out_specs=block,
            scratch_shapes=[
                pltpu.VMEM((count, depth, lanes), jnp.float32),
                pltpu.VMEM((count, depth, lanes), jnp.float32),
            ],
        ),
        out_shape=jax.ShapeDtypeStruct(vertex.shape, jnp.float32),
        input_output_aliases={7: 0} if held else {},
        compiler_params=pltpu.CompilerParams(vmem_limit_bytes=vmem_bytes),
        cost_estimate=cost(10),
        name="crossed",
    )(*operands)


def coupling_matrices(neighbours, pair_count):
    shards = lax.axis_size("pair")
    own = lax.axis_index("pair")
    pair_column = neighbours[:, 0]
    partner_column = neighbours[:, 1]
    sign_column = neighbours[:, 2]
    inner = lax.iota(jnp.int32, pair_count)
    left_ids = jnp.concatenate([(own ^ j) * pair_count + inner for j in range(shards)])
    right_ids = own * pair_count + inner
    partner_hits = (partner_column[:, None] == left_ids[None, :]).astype(jnp.bfloat16)
    pair_hits = jnp.where(
        pair_column[:, None] == right_ids[None, :], sign_column[:, None], 0
    ).astype(jnp.bfloat16)
    signs = lax.dot_general(
        partner_hits, pair_hits, (((0,), (0,)), ((), ())), preferred_element_type=jnp.float32
    )
    return signs.astype(jnp.bfloat16).reshape(shards, pair_count, pair_count)


def body(vertex, bubble, stencil, freq_map, neighbours):
    slots, components, width, depth, pairs = vertex.shape
    rows = freq_map
    places = lax.iota(jnp.int32, width)
    shards = lax.axis_size("pair")
    devices = lax.axis_size("freq")
    onward = [(i, i + 1) for i in range(devices - 1)]
    backward = [(i + 1, i) for i in range(devices - 1)]
    across = [(i, i ^ 2) for i in range(shards)]
    beside = [(i, i ^ 1) for i in range(shards)]

    partners = []
    for slot in range(slots):
        spin = vertex[slot, 0]
        far = lax.ppermute(spin, "pair", across)
        near = lax.ppermute(spin, "pair", beside)
        partners.append((near, far, lax.ppermute(far, "pair", beside)))
    chunks = [(1, 0), (1, 1), (0, 0), (0, 1)]
    sides = {}
    for component, half in chunks:
        packed = pack(vertex, rows, component, half)
        sides[component, half] = (
            lax.ppermute(packed, "freq", onward),
            lax.ppermute(packed, "freq", backward),
        )
    scaled = jnp.broadcast_to(
        (step_size * bubble)[:, :, None], (slots, depth, lanes)
    )
    coupling = coupling_matrices(neighbours, pairs)
    section = None
    for component, half in chunks:
        if (component, half) == (0, 0):
            for slot in range(slots):
                section = lattice(vertex, slot, partners[slot], coupling, scaled, section)
        section = crossed(
            vertex, rows, places, stencil, *sides[component, half], scaled, component, half,
            component == 0, section,
        )
    return section


def solution(mesh):
    in_specs = (P("freq", None, None, None, "pair"), P("freq", None), P("freq", None), P(), P())
    out_specs = P("freq", None, None, None, "pair")
    return jax.shard_map(body, mesh=mesh, in_specs=in_specs, out_specs=out_specs, check_vma=False)
```

time: 730 us -> 334 us (0.46); the launches traced: 719 us -> 333 us
  waiting for transfers between devices: 360 us -> 163 us
  matrix products: 192 us -> 12.1 us
  Pallas kernels: 0 us -> 100 us
  local copies, waits for them, and re-layouts: 107 us -> 11.9 us
  other arithmetic: 37 us -> 0.02 us
  starting transfers between devices: 8.98 us -> 44.8 us
  between operations: 13.9 us -> 0.26 us
    ppermute x2 -> x14, waiting for transfers between devices: 360 us -> 163 us  [the longest x4 76.6 us: body(): lax.ppermute(packed, 'freq', onward)]
    dot_general x5 -> x1, matrix products: 192 us -> 12.1 us  [coupling_matrices(): lax.dot_general(partner_hits, pair_hits, (((0,), (0,)), ((), ())), prefer...]
    pallas_call x0 -> x10, Pallas kernels: none -> 100 us  [the longest x4 60.1 us: crossed(): pl.pallas_call(functools.partial(crossed_kernel, has_base), grid_spec=plt...]
    dot_general x4 -> x0, local copies, waits for them, and re-layouts: 62 us -> none  [the longest x1 20.5 us: body(): mapped = jnp.einsum('nm,scmwp->scnwp', selector, mixed, precision=highest)]
    ppermute x2 -> x14, starting transfers between devices: 8.98 us -> 44.8 us  [the longest x4 29.2 us: body(): lax.ppermute(packed, 'freq', backward)]
    unnamed x11 -> x22, local copies, waits for them, and re-layouts: 39.5 us -> 6.87 us
    add x3 -> x2, other arithmetic: 30.1 us -> 0.01 us  [coupling_matrices(): (own ^ j) * pair_count + inner]
  transfers between devices with their start and end apart: 3 -> 14, of which waited for: 2 -> 6; matrix products, arithmetic and copies ran while one was open for 20% -> 5% of each run, Pallas kernels for 0% -> 25%
where the time goes in v1:
time: 334 us; the launch traced here: 333 us
  waiting for transfers between devices  163 us (49%)
  Pallas kernels  100 us (30%)
  starting transfers between devices  44.8 us (13%)
  matrix products  12.1 us (4%)
  local copies, waits for them, and re-layouts  11.9 us (4%)
    ppermute x4, waiting for transfers between devices, body(): lax.ppermute(packed, 'freq', onward)  76.6 us
    pallas_call x4, Pallas kernels, crossed(): pl.pallas_call(functools.partial(crossed_kernel, has_base), grid_spec=plt...  60.1 us
    ppermute x2, waiting for transfers between devices, body(): far = lax.ppermute(spin, 'pair', across)  46.2 us
    ppermute x4, waiting for transfers between devices, body(): lax.ppermute(packed, 'freq', backward)  40.6 us
    ppermute x4, starting transfers between devices, body(): lax.ppermute(packed, 'freq', backward)  29.2 us
    pallas_call x2, Pallas kernels, lattice(): pl.pallas_call(lattice_kernel, grid=(width // row_group,), in_specs=[pl.B...  28.9 us
    dot_general x1, matrix products, coupling_matrices(): lax.dot_general(partner_hits, pair_hits, (((0,), (0,)), ((), ())), prefer...  12.1 us
    pallas_call x4, Pallas kernels, pack(): pl.pallas_call(pack_kernel, grid_spec=pltpu.PrefetchScalarGridSpec(num_sc...  11.2 us
  transfers between devices with their start and end apart: 14, of which 6 were waited for; matrix products, arithmetic and copies ran while one was open for 5% of the time, Pallas kernels for 25%

profile of v1, /device:TPU:24, one launch (start us, length us, event | category | flops | bytes accessed | tf_op | source)
XLA Modules:
  0.0 332.9 jit_solution(18356963063914266676)
XLA Ops:
  0.7 2.5 pack.7
  3.2 3.8 %collective-permute-start.12 = (f32[2,48,48,128]{3,2,1,0:T(8,128)S(1)}, f32[2,48,48,128]{3,2,1,0:T(8,128)S(1)}, u32[]{:S(2)}, u32[]{:S(2)}) collective-permute-start(f32[2,48,48,128]{3,2,1,0:T(8,128)S(1)} %pack.7), channel_id=1, source_target_pairs={{0,4},{4,8},{8,12},{12,16},{16,20},{20,24},{24,28},{28,32},{32,36}... | collective-permute-start | bytes 7077896 | tf_op jit(solution)/shard_map/ppermute | solution.py:248
  7.0 5.1 %collective-permute-start.13 = (f32[2,48,48,128]{3,2,1,0:T(8,128)S(1)}, f32[2,48,48,128]{3,2,1,0:T(8,128)S(1)}, u32[]{:S(2)}, u32[]{:S(2)}) collective-permute-start(f32[2,48,48,128]{3,2,1,0:T(8,128)S(1)} %pack.7), channel_id=1, source_target_pairs={{4,0},{8,4},{12,8},{16,12},{20,16},{24,20},{28,24},{32,28},{36,32}... | collective-permute-start | bytes 7077896 | tf_op jit(solution)/shard_map/ppermute | solution.py:249
  12.2 3.6 %pack.6 = f32[2,48,48,128]{3,2,1,0:T(8,128)} custom-call(s32[48]{0:T(128)S(1)} %copy-done.7, f32[2,2,48,48,256]{4,3,2,1,0:T(8,128)} %vertex.15), custom_call_target="tpu_custom_call" | custom-call | bytes 9000000 | tf_op jit(solution)/shard_map/pack/pallas_call | solution.py:49
  15.8 1.9 collective-permute-start.10
  17.7 4.9 %slice_bitcast_fusion = (f32[48,48,256]{2,1,0:T(8,128)}, f32[48,48,256]{2,1,0:T(8,128)}) fusion(f32[2,2,48,48,256]{4,3,2,1,0:T(8,128)} %vertex.15), kind=kLoop, calls=%fused_computation.9 | loop fusion | bytes 9437184 | tf_op jit(solution)/shard_map/squeeze | solution.py:239
  22.6 2.9 collective-permute-start.8
  25.5 6.3 %collective-permute-start.11 = (f32[2,48,48,128]{3,2,1,0:T(8,128)}, f32[2,48,48,128]{3,2,1,0:T(8,128)}, u32[]{:S(2)}, u32[]{:S(2)}) collective-permute-start(f32[2,48,48,128]{3,2,1,0:T(8,128)} %pack.6), channel_id=1, source_target_pairs={{4,0},{8,4},{12,8},{16,12},{20,16},{24,20},{28,24},{32,28},{36,32}... | collective-permute-start | bytes 7077896 | tf_op jit(solution)/shard_map/ppermute | solution.py:249
  31.8 30.5 %collective-permute-done.12.before = f32[2,48,48,128]{3,2,1,0:T(8,128)S(1)} collective-permute-done((f32[2,48,48,128]{3,2,1,0:T(8,128)S(1)}, f32[2,48,48,128]{3,2,1,0:T(8,128)S(1)}, u32[]{:S(2)}, u32[]{:S(2)}) %collective-permute-start.12) | collective-permute-done | bytes 2359328 | tf_op jit(solution)/shard_map/ppermute | solution.py:248
  62.3 1.5 collective-permute-done.13.after
  63.8 2.9 collective-permute-start.5
  66.8 46.1 %collective-permute-done.10.before = f32[2,48,48,128]{3,2,1,0:T(8,128)S(1)} collective-permute-done((f32[2,48,48,128]{3,2,1,0:T(8,128)}, f32[2,48,48,128]{3,2,1,0:T(8,128)S(1)}, u32[]{:S(2)}, u32[]{:S(2)}) %collective-permute-start.10) | collective-permute-done | bytes 2359328 | tf_op jit(solution)/shard_map/ppermute | solution.py:248
  112.9 5.0 %collective-permute-done.8.partner_2 = f32[48,48,256]{2,1,0:T(8,128)} collective-permute-done((f32[48,48,256]{2,1,0:T(8,128)}, f32[48,48,256]{2,1,0:T(8,128)}, u32[]{:S(2)}, u32[]{:S(2)}) %collective-permute-start.8) | collective-permute-done | bytes 2359328 | tf_op jit(solution)/shard_map/ppermute | solution.py:240
  117.9 2.5 pack.5
  120.5 1.4 copy-done.5
  121.9 2.5 pack.4
  124.5 1.4 copy-done.4
  125.9 39.1 %collective-permute-done.11.after = f32[2,48,48,128]{3,2,1,0:T(8,128)} collective-permute-done((f32[2,48,48,128]{3,2,1,0:T(8,128)}, f32[2,48,48,128]{3,2,1,0:T(8,128)}, u32[]{:S(2)}, u32[]{:S(2)}) %collective-permute-start.11) | collective-permute-done | bytes 2359328 | tf_op jit(solution)/shard_map/ppermute | solution.py:249
  165.0 1.9 collective-permute-start.2
  167.0 10.8 %collective-permute-start.3 = (f32[2,48,48,128]{3,2,1,0:T(8,128)}, f32[2,48,48,128]{3,2,1,0:T(8,128)}, u32[]{:S(2)}, u32[]{:S(2)}) collective-permute-start(f32[2,48,48,128]{3,2,1,0:T(8,128)} %copy-done.5), channel_id=1, source_target_pairs={{4,0},{8,4},{12,8},{16,12},{20,16},{24,20},{28,24},{32,28},{36,32}... | collective-permute-start | bytes 7077896 | tf_op jit(solution)/shard_map/ppermute | solution.py:249
  177.8 41.2 %collective-permute-done.5.partner_2 = f32[48,48,256]{2,1,0:T(8,128)} collective-permute-done((f32[48,48,256]{2,1,0:T(8,128)}, f32[48,48,256]{2,1,0:T(8,128)}, u32[]{:S(2)}, u32[]{:S(2)}) %collective-permute-start.5) | collective-permute-done | bytes 2359328 | tf_op jit(solution)/shard_map/ppermute | solution.py:240
  219.0 1.9 collective-permute-start
  220.9 6.9 %collective-permute-start.1 = (f32[2,48,48,128]{3,2,1,0:T(8,128)}, f32[2,48,48,128]{3,2,1,0:T(8,128)}, u32[]{:S(2)}, u32[]{:S(2)}) collective-permute-start(f32[2,48,48,128]{3,2,1,0:T(8,128)} %copy-done.4), channel_id=1, source_target_pairs={{4,0},{8,4},{12,8},{16,12},{20,16},{24,20},{28,24},{32,28},{36,32}... | collective-permute-start | bytes 7077896 | tf_op jit(solution)/shard_map/ppermute | solution.py:249
  228.2 12.1 %fusion.8 = bf16[1024,256]{1,0:T(8,128)(2,1)S(1)} fusion(s32[8192]{0:T(1024)S(1)} %bitcast.11, s32[256]{0:T(256)S(1)} %get-tuple-element.13, s32[8192]{0:T(1024)S(1)} %bitcast.12, s32[1024]{0:T(1024)S(1)} %pad_add_fusion, s32[8192]{0:T(1024)S(1)} %bitcast.10), kind=kOutput, calls=%fused_computation.11 | convolution fusion | flops 4309909504 | bytes 627712 | tf_op jit(solution)/shard_map/dot_general | solution.py:220
  240.5 1.7 copy-done.1
  242.1 1.7 copy-done.3
  243.8 14.1 %crossed.4.rest_0_ = f32[2,2,48,48,256]{4,3,2,1,0:T(8,128)} custom-call(s32[48]{0:T(128)S(1)} %copy-done.7, s32[48]{0:T(128)S(1)} %iota.27.places, f32[2,5]{1,0:T(2,128)S(1)} %copy-done.8, f32[2,2,48,48,256]{4,3,2,1,0:T(8,128)} %vertex.15, f32[2,48,48,128]{3,2,1,0:T(8,128)S(1)} %copy-done.1, f32[2,48,48,128]{3,2,1,0:T(8,128)S(1)} %copy-done.3, ...), custom_call_target="tpu_custom_call" | custom-call | bytes 30000000 | tf_op jit(solution)/shard_map/crossed/pallas_call | solution.py:178
  257.9 14.6 %crossed.5.base = f32[2,2,48,48,256]{4,3,2,1,0:T(8,128)} custom-call(s32[48]{0:T(128)S(1)} %copy-done.7, s32[48]{0:T(128)S(1)} %iota.26.places, f32[2,5]{1,0:T(2,128)S(1)} %copy-done.8, f32[2,2,48,48,256]{4,3,2,1,0:T(8,128)} %vertex.15, f32[2,48,48,128]{3,2,1,0:T(8,128)S(1)} %collective-permute-done.10.before, ...), custom_call_target="tpu_custom_call", output_to_operand_aliasing={{}: (7, {})} | custom-call | bytes 30000000 | tf_op jit(solution)/shard_map/crossed/pallas_call | solution.py:178
  272.5 14.4 %lattice.2.base = f32[2,2,48,48,256]{4,3,2,1,0:T(8,128)} custom-call(f32[2,2,48,48,256]{4,3,2,1,0:T(8,128)} %vertex.15, f32[48,48,256]{2,1,0:T(8,128)} %collective-permute-done.7.partner_1, f32[48,48,256]{2,1,0:T(8,128)} %collective-permute-done.8.partner_2, f32[48,48,256]{2,1,0:T(8,128)} %collective-permute-done.9.partner_3, ...), custom_call_target="tpu_custom_call", output_to_operand_aliasing={{}: (7, {})} | custom-call | bytes 30000000 | tf_op jit(solution)/shard_map/lattice/pallas_call | solution.py:94
  287.0 14.5 %lattice.3.rest_0_ = f32[2,2,48,48,256]{4,3,2,1,0:T(8,128)} custom-call(f32[2,2,48,48,256]{4,3,2,1,0:T(8,128)} %vertex.15, f32[48,48,256]{2,1,0:T(8,128)} %collective-permute-done.4.partner_1, f32[48,48,256]{2,1,0:T(8,128)} %collective-permute-done.5.partner_2, f32[48,48,256]{2,1,0:T(8,128)} %collective-permute-done.6.partner_3, ...), custom_call_target="tpu_custom_call", output_to_operand_aliasing={{}: (7, {})} | custom-call | bytes 30000000 | tf_op jit(solution)/shard_map/lattice/pallas_call | solution.py:94
  301.4 15.7 %crossed.6.rest_0_ = f32[2,2,48,48,256]{4,3,2,1,0:T(8,128)} custom-call(s32[48]{0:T(128)S(1)} %copy-done.7, s32[48]{0:T(128)S(1)} %iota.21.places, f32[2,5]{1,0:T(2,128)S(1)} %copy-done.8, f32[2,2,48,48,256]{4,3,2,1,0:T(8,128)} %vertex.15, f32[2,48,48,128]{3,2,1,0:T(8,128)} %collective-permute-done.2.before, ...), custom_call_target="tpu_custom_call", output_to_operand_aliasing={{}: (7, {})} | custom-call | bytes 30000000 | tf_op jit(solution)/shard_map/crossed/pallas_call | solution.py:178
  317.2 15.7 %crossed.7 = f32[2,2,48,48,256]{4,3,2,1,0:T(8,128)} custom-call(s32[48]{0:T(128)S(1)} %copy-done.7, s32[48]{0:T(128)S(1)} %iota.20.places, f32[2,5]{1,0:T(2,128)S(1)} %copy-done.8, f32[2,2,48,48,256]{4,3,2,1,0:T(8,128)} %vertex.15, f32[2,48,48,128]{3,2,1,0:T(8,128)} %collective-permute-done.before, ...), custom_call_target="tpu_custom_call", output_to_operand_aliasing={{}: (7, {})} | custom-call | bytes 30000000 | tf_op jit(solution)/shard_map/crossed/pallas_call | solution.py:178
  (40 shorter events, 1.2 us)
Async XLA Ops:
  0.0 0.7 copy-start.6
  0.7 11.5 %copy-start.7 = (s32[48]{0:T(128)S(1)}, s32[48]{0:T(128)}, u32[]{:S(2)}) copy-start(s32[48]{0:T(128)} %rows.15) | copy-start | bytes 580
  3.2 59.1 %collective-permute-start.12 = (f32[2,48,48,128]{3,2,1,0:T(8,128)S(1)}, f32[2,48,48,128]{3,2,1,0:T(8,128)S(1)}, u32[]{:S(2)}, u32[]{:S(2)}) collective-permute-start(f32[2,48,48,128]{3,2,1,0:T(8,128)S(1)} %pack.7), channel_id=1, source_target_pairs={{0,4},{4,8},{8,12},{12,16},{16,20},{20,24},{24,28},{28,32},{32,36}... | collective-permute-start | bytes 7077896 | tf_op jit(solution)/shard_map/ppermute | solution.py:248
  7.0 56.8 %collective-permute-start.13 = (f32[2,48,48,128]{3,2,1,0:T(8,128)S(1)}, f32[2,48,48,128]{3,2,1,0:T(8,128)S(1)}, u32[]{:S(2)}, u32[]{:S(2)}) collective-permute-start(f32[2,48,48,128]{3,2,1,0:T(8,128)S(1)} %pack.7), channel_id=1, source_target_pairs={{4,0},{8,4},{12,8},{16,12},{20,16},{24,20},{28,24},{32,28},{36,32}... | collective-permute-start | bytes 7077896 | tf_op jit(solution)/shard_map/ppermute | solution.py:249
  15.8 97.1 %collective-permute-start.10 = (f32[2,48,48,128]{3,2,1,0:T(8,128)}, f32[2,48,48,128]{3,2,1,0:T(8,128)S(1)}, u32[]{:S(2)}, u32[]{:S(2)}) collective-permute-start(f32[2,48,48,128]{3,2,1,0:T(8,128)} %pack.6), channel_id=1, source_target_pairs={{0,4},{4,8},{8,12},{12,16},{16,20},{20,24},{24,28},{28,32},{32,36}... | collective-permute-start | bytes 7077896 | tf_op jit(solution)/shard_map/ppermute | solution.py:248
  22.6 95.2 %collective-permute-start.8 = (f32[48,48,256]{2,1,0:T(8,128)}, f32[48,48,256]{2,1,0:T(8,128)}, u32[]{:S(2)}, u32[]{:S(2)}) collective-permute-start(f32[48,48,256]{2,1,0:T(8,128)} %get-tuple-element.5), channel_id=1, source_target_pairs={{0,2},{1,3},{2,0},{3,1},{4,6},{5,7},{6,4},{7,5},{8,10},{9,11},{10,... | collective-permute-start | bytes 7077896 | tf_op jit(solution)/shard_map/ppermute | solution.py:240
  25.5 139.5 %collective-permute-start.11 = (f32[2,48,48,128]{3,2,1,0:T(8,128)}, f32[2,48,48,128]{3,2,1,0:T(8,128)}, u32[]{:S(2)}, u32[]{:S(2)}) collective-permute-start(f32[2,48,48,128]{3,2,1,0:T(8,128)} %pack.6), channel_id=1, source_target_pairs={{4,0},{8,4},{12,8},{16,12},{20,16},{24,20},{28,24},{32,28},{36,32}... | collective-permute-start | bytes 7077896 | tf_op jit(solution)/shard_map/ppermute | solution.py:249
  62.3 58.1 %copy-start = (f32[2,48,48,128]{3,2,1,0:T(8,128)}, f32[2,48,48,128]{3,2,1,0:T(8,128)S(1)}, u32[]{:S(2)}) copy-start(f32[2,48,48,128]{3,2,1,0:T(8,128)S(1)} %collective-permute-done.12.before) | copy-start | bytes 7077892
  62.3 104.6 %collective-permute-start.7 = (f32[48,48,256]{2,1,0:T(8,128)}, f32[48,48,256]{2,1,0:T(8,128)}, u32[]{:S(2)}, u32[]{:S(2)}) collective-permute-start(f32[48,48,256]{2,1,0:T(8,128)} %get-tuple-element.5), channel_id=1, source_target_pairs={{0,1},{1,0},{2,3},{3,2},{4,5},{5,4},{6,7},{7,6},{8,9},{9,8},{10,11... | collective-permute-start | bytes 7077896 | tf_op jit(solution)/shard_map/ppermute | solution.py:241
  63.8 56.6 %copy-start.2 = (f32[2,48,48,128]{3,2,1,0:T(8,128)}, f32[2,48,48,128]{3,2,1,0:T(8,128)S(1)}, u32[]{:S(2)}) copy-start(f32[2,48,48,128]{3,2,1,0:T(8,128)S(1)} %collective-permute-done.13.after) | copy-start | bytes 7077892
  63.8 155.2 %collective-permute-start.5 = (f32[48,48,256]{2,1,0:T(8,128)}, f32[48,48,256]{2,1,0:T(8,128)}, u32[]{:S(2)}, u32[]{:S(2)}) collective-permute-start(f32[48,48,256]{2,1,0:T(8,128)} %get-tuple-element.6), channel_id=1, source_target_pairs={{0,2},{1,3},{2,0},{3,1},{4,6},{5,7},{6,4},{7,5},{8,10},{9,11},{10,... | collective-permute-start | bytes 7077896 | tf_op jit(solution)/shard_map/ppermute | solution.py:240
  112.9 108.0 %collective-permute-start.4 = (f32[48,48,256]{2,1,0:T(8,128)}, f32[48,48,256]{2,1,0:T(8,128)}, u32[]{:S(2)}, u32[]{:S(2)}) collective-permute-start(f32[48,48,256]{2,1,0:T(8,128)} %get-tuple-element.6), channel_id=1, source_target_pairs={{0,1},{1,0},{2,3},{3,2},{4,5},{5,4},{6,7},{7,6},{8,9},{9,8},{10,11... | collective-permute-start | bytes 7077896 | tf_op jit(solution)/shard_map/ppermute | solution.py:241
  117.9 110.0 %collective-permute-start.9 = (f32[48,48,256]{2,1,0:T(8,128)}, f32[48,48,256]{2,1,0:T(8,128)}, u32[]{:S(2)}, u32[]{:S(2)}) collective-permute-start(f32[48,48,256]{2,1,0:T(8,128)} %collective-permute-done.8.partner_2), channel_id=1, source_target_pairs={{0,1},{1,0},{2,3},{3,2},{4,5},{5,4},{6,7},{7,6},{8,9},{9,8},{10,11... | collective-permute-start | bytes 7077896 | tf_op jit(solution)/shard_map/ppermute | solution.py:242
  120.4 1.4 copy-start.5
  121.9 4.0 %copy-start.10 = (f32[2,48]{1,0:T(2,128)S(1)}, f32[2,48]{1,0:T(2,128)}, u32[]{:S(2)}) copy-start(f32[2,48]{1,0:T(2,128)} %param.6) | copy-start | bytes 1156
  121.9 106.3 %copy-start.9 = (s32[8192,3]{0,1:T(4,128)S(1)}, s32[8192,3]{0,1:T(4,128)}, u32[]{:S(2)}) copy-start(s32[8192,3]{0,1:T(4,128)} %param.9) | copy-start | bytes 294916
  124.4 1.4 copy-start.4
  165.0 136.4 %collective-permute-start.2 = (f32[2,48,48,128]{3,2,1,0:T(8,128)}, f32[2,48,48,128]{3,2,1,0:T(8,128)}, u32[]{:S(2)}, u32[]{:S(2)}) collective-permute-start(f32[2,48,48,128]{3,2,1,0:T(8,128)} %copy-done.5), channel_id=1, source_target_pairs={{0,4},{4,8},{8,12},{12,16},{16,20},{20,24},{24,28},{28,32},{32,36}... | collective-permute-start | bytes 7077896 | tf_op jit(solution)/shard_map/ppermute | solution.py:248
  167.0 134.5 %collective-permute-start.3 = (f32[2,48,48,128]{3,2,1,0:T(8,128)}, f32[2,48,48,128]{3,2,1,0:T(8,128)}, u32[]{:S(2)}, u32[]{:S(2)}) collective-permute-start(f32[2,48,48,128]{3,2,1,0:T(8,128)} %copy-done.5), channel_id=1, source_target_pairs={{4,0},{8,4},{12,8},{16,12},{20,16},{24,20},{28,24},{32,28},{36,32}... | collective-permute-start | bytes 7077896 | tf_op jit(solution)/shard_map/ppermute | solution.py:249
  219.0 98.2 %collective-permute-start = (f32[2,48,48,128]{3,2,1,0:T(8,128)}, f32[2,48,48,128]{3,2,1,0:T(8,128)}, u32[]{:S(2)}, u32[]{:S(2)}) collective-permute-start(f32[2,48,48,128]{3,2,1,0:T(8,128)} %copy-done.4), channel_id=1, source_target_pairs={{0,4},{4,8},{8,12},{12,16},{16,20},{20,24},{24,28},{28,32},{32,36}... | collective-permute-start | bytes 7077896 | tf_op jit(solution)/shard_map/ppermute | solution.py:248
  220.9 96.2 %collective-permute-start.1 = (f32[2,48,48,128]{3,2,1,0:T(8,128)}, f32[2,48,48,128]{3,2,1,0:T(8,128)}, u32[]{:S(2)}, u32[]{:S(2)}) collective-permute-start(f32[2,48,48,128]{3,2,1,0:T(8,128)} %copy-done.4), channel_id=1, source_target_pairs={{4,0},{8,4},{12,8},{16,12},{20,16},{24,20},{28,24},{32,28},{36,32}... | collective-permute-start | bytes 7077896 | tf_op jit(solution)/shard_map/ppermute | solution.py:249
  227.9 59.1 %collective-permute-start.6 = (f32[48,48,256]{2,1,0:T(8,128)}, f32[48,48,256]{2,1,0:T(8,128)}, u32[]{:S(2)}, u32[]{:S(2)}) collective-permute-start(f32[48,48,256]{2,1,0:T(8,128)} %collective-permute-done.5.partner_2), channel_id=1, source_target_pairs={{0,1},{1,0},{2,3},{3,2},{4,5},{5,4},{6,7},{7,6},{8,9},{9,8},{10,11... | collective-permute-start | bytes 7077896 | tf_op jit(solution)/shard_map/ppermute | solution.py:242
  228.2 12.2 %copy-start.8 = (f32[2,5]{1,0:T(2,128)S(1)}, f32[2,5]{1,0:T(2,128)}, u32[]{:S(2)}) copy-start(f32[2,5]{1,0:T(2,128)} %stencil.7) | copy-start | bytes 124
  240.5 1.7 copy-start.1
  242.1 1.7 copy-start.3
